TPU v7x, 32 devices: a whole 2x2x4 slice. The times are simulated.
32 devices in a mesh: gx: 2 (over core), gy: 4 (over z), gz: 4 (over y, x).
Axes of the slice: x: 2, y: 2, z: 4, core: 2. Of those that a mesh axis runs over, the one named last changes fastest.
Arguments:
- residual: float32 [32, 64, 1024], P('gx', 'gy', 'gz'), may hold values from -6 to 6
- fdm_vectors: bfloat16 [2, 4, 4, 3, 10, 10, 128], P('gx', 'gy', 'gz'), may hold values from -2 to 2
- fdm_eigen: float32 [2, 4, 4, 3, 10, 128], P('gx', 'gy', 'gz'), may hold values from 0.1 to 4
- coarse_basis: float32 [8, 8, 8], replicated, may hold values from -0.75 to 0.75
- x_interior: float32 [2, 4, 4, 16, 16], P('gx', 'gy', 'gz'), may hold values from -1.5 to 1.5
- x_separator: float32 [2, 4, 4, 5, 16, 256], P('gx', 'gy', 'gz'), may hold values from -0.375 to 0.375
Outputs:
- preconditioned: float32 [32, 64, 1024], P('gx', 'gy', 'gz')
All inputs are finite; a program needn't handle non-finite values.
Results may differ from a plain program's by a relative error of at most 0.0003.
Values sent between devices are 32-bit elements; how exact they have to be, the bound alone decides.
A program may use at most 128 MiB of HBM per device.

v0:
```python
import functools

import jax
import jax.numpy as jnp
import numpy as np
from jax import lax
from jax.experimental import pallas as pl
from jax.experimental.pallas import tpu as pltpu
from jax.sharding import PartitionSpec as P

PTS = 8
EXT = PTS + 2
ROWS = 16
HIGHEST = lax.Precision.HIGHEST
F32 = jnp.float32
BF16 = jnp.bfloat16


def selection(groups, count):
    lanes = groups * count
    size = count * PTS
    matrix = np.zeros((groups * size + 128, EXT * lanes), np.float32)
    for g in range(groups):
        for r in range(count):
            for k in range(EXT):
                z = PTS * r + k - 1
                row = g * size + z
                if z < 0:
                    row = groups * size + 2 * g
                elif z >= size:
                    row = groups * size + 2 * g + 1
                matrix[row, k * lanes + g * count + r] = 1
    return matrix


def halves(value):
    high = value.astype(BF16)
    return high, (value - high.astype(F32)).astype(BF16)


def prepare_modes(vec_ref, eig_ref, modes, lam, lamx):
    def spread(n, _):
        d, i = n // EXT, n % EXT
        rows = vec_ref[d, i].astype(F32)
        for a in range(EXT):
            modes[pl.ds(pl.multiple_of((n * EXT + a) * 8, 8), 8), :] = jnp.broadcast_to(rows[a : a + 1], (8, 128))
        return 0

    lax.fori_loop(0, 3 * EXT, spread, 0)
    for d in range(2):
        rows = eig_ref[d + 1]
        for a in range(EXT):
            lam[(d * EXT + a) * 8 : (d * EXT + a + 1) * 8, :] = jnp.broadcast_to(rows[a : a + 1], (8, 128))
    lamx[...] = jnp.ones_like(lamx)
    lamx[0:EXT, :] = eig_ref[0]


def gather_elements(grid_ref, ends_ref, sel_ref, parts, buf, ex, ey):
    groups = ex * ey
    size = grid_ref.shape[2]
    rows = EXT * ROWS
    ends = None
    for g in range(groups):
        x, y = PTS * (g // ey), PTS * (g % ey)
        block = grid_ref[x : x + EXT, y : y + ROWS, :].reshape(rows, size)
        high, low = halves(block)
        parts[0:rows, g * size : (g + 1) * size] = high
        parts[rows : 2 * rows, g * size : (g + 1) * size] = low
        side = ends_ref[x : x + EXT, y : y + ROWS, :].reshape(rows, 128)
        side = side if g == 0 else pltpu.roll(side, 2 * g, 1)
        ends = side if ends is None else ends + side
    high, low = halves(ends)
    width = groups * size
    parts[0:rows, width : width + 128] = high
    parts[rows : 2 * rows, width : width + 128] = low
    for pair in range(EXT // 2):
        columns = slice(pair * 256, (pair + 1) * 256)
        both = jnp.dot(parts[:, 0:width], sel_ref[0:width, columns], preferred_element_type=F32)
        if pair in (0, EXT // 2 - 1):
            both = both + jnp.dot(
                parts[:, width : width + 128], sel_ref[width : width + 128, columns], preferred_element_type=F32
            )
        total = both[0:rows] + both[rows : 2 * rows]
        buf[2 * pair * rows : (2 * pair + 1) * rows, :] = total[:, 0:128]
        buf[(2 * pair + 1) * rows : (2 * pair + 2) * rows, :] = total[:, 128:256]


def contract(values, modes, d, back):
    out = []
    for p in range(EXT):
        total = None
        for q in range(EXT):
            i, a = (p, q) if back else (q, p)
            start = ((d * EXT + i) * EXT + a) * 8
            term = modes[start : start + 8, :][None] * values[q]
            total = term if total is None else total + term
        out.append(total)
    return out


def tile(ref, start):
    return ref[pl.ds(start, ROWS), :].reshape(2, 8, 128)


def put(ref, start, value):
    ref[pl.ds(start, ROWS), :] = value.reshape(ROWS, 128)


def along_z(buf, modes, back):
    def body(i, _):
        at = [pl.multiple_of((k * EXT + i) * ROWS, ROWS) for k in range(EXT)]
        out = contract([tile(buf, s) for s in at], modes, 2, back)
        for s, value in zip(at, out):
            put(buf, s, value)
        return 0

    lax.fori_loop(0, EXT, body, 0)


def along_xy(buf, turn, modes, lam, lamx):
    def body(c, _):
        at = [pl.multiple_of((c * EXT + i) * ROWS, ROWS) for i in range(EXT)]
        t = contract([tile(buf, s) for s in at], modes, 0, False)
        for a in range(EXT):
            turn[a * ROWS : (a + 1) * ROWS, :] = t[a].reshape(ROWS, 128)
        t = [turn[pl.ds(j, ROWS, ROWS), :].reshape(2, 8, 128) for j in range(EXT)]
        t = contract(t, modes, 1, False)
        first = lamx[...].reshape(2, 8, 128)
        third = lam[pl.ds(pl.multiple_of((EXT + c) * 8, 8), 8), :][None]
        t = [v / (first + lam[b * 8 : (b + 1) * 8, :][None] + third) for b, v in enumerate(t)]
        t = contract(t, modes, 1, True)
        for j in range(EXT):
            turn[j * ROWS : (j + 1) * ROWS, :] = t[j].reshape(ROWS, 128)
        t = [turn[pl.ds(a, ROWS, ROWS), :].reshape(2, 8, 128) for a in range(EXT)]
        t = contract(t, modes, 0, True)
        for s, value in zip(at, t):
            put(buf, s, value)
        return 0

    lax.fori_loop(0, EXT, body, 0)


def scatter_elements(buf, sel_ref, parts, grid_ref, ends_ref, ex, ey):
    groups = ex * ey
    size = grid_ref.shape[2]
    rows = EXT * ROWS
    lanes = EXT * 128
    for k in range(EXT):
        high, low = halves(buf[k * rows : (k + 1) * rows, :])
        parts[0:rows, k * 128 : (k + 1) * 128] = high
        parts[rows : 2 * rows, k * 128 : (k + 1) * 128] = low
    dims = (((1,), (1,)), ((), ()))
    grid_ref[...] = jnp.zeros_like(grid_ref)
    ends_ref[...] = jnp.zeros_like(ends_ref)
    width = groups * size
    both = lax.dot_general(
        parts[:, 0:lanes], sel_ref[width : width + 128, :], dims, preferred_element_type=F32
    )
    ends = both[0:rows] + both[rows : 2 * rows]
    lane = lax.broadcasted_iota(jnp.int32, (1, 128), 1)
    for g in range(groups):
        x, y = PTS * (g // ey), PTS * (g % ey)
        both = lax.dot_general(
            parts[:, 0:lanes], sel_ref[g * size : (g + 1) * size, :], dims, preferred_element_type=F32
        )
        total = (both[0:rows] + both[rows : 2 * rows]).reshape(EXT, ROWS, size)
        grid_ref[x : x + EXT, y : y + EXT, :] += total[:, 0:EXT]
        side = ends if g == 0 else pltpu.roll(ends, 128 - 2 * g, 1)
        side = jnp.where(lane < 2, side, 0.0).reshape(EXT, ROWS, 128)
        ends_ref[x : x + EXT, y : y + EXT, :] += side[:, 0:EXT]


def smooth_kernel(ex, ey, grid_in, ends_in, vec, eig, sel, grid_out, ends_out, parts, buf, turn, modes, lam, lamx):
    turn[...] = jnp.zeros_like(turn)
    prepare_modes(vec, eig, modes, lam, lamx)
    gather_elements(grid_in, ends_in, sel, parts, buf, ex, ey)
    along_z(buf, modes, False)
    along_xy(buf, turn, modes, lam, lamx)
    along_z(buf, modes, True)
    scatter_elements(buf, sel, parts, grid_out, ends_out, ex, ey)


def smooth_call(padded, vectors, eigen, ex, ey, ez):
    nx, ny, nz = padded.shape
    size = nz - 2
    tall = PTS * (ey - 1) + ROWS
    sel = jnp.asarray(selection(ex * ey, ez), BF16)
    grid = jnp.pad(padded[:, :, 1:-1], ((0, 0), (0, tall - ny), (0, 0)))
    ends = jnp.stack([padded[:, :, 0], padded[:, :, -1]], -1)
    ends = jnp.pad(ends, ((0, 0), (0, tall - ny), (0, 126)))
    vmem = pl.BlockSpec(memory_space=pltpu.VMEM)
    rows = EXT * ROWS
    out, sides = pl.pallas_call(
        functools.partial(smooth_kernel, ex, ey),
        out_shape=(
            jax.ShapeDtypeStruct((nx, tall, size), F32),
            jax.ShapeDtypeStruct((nx, tall, 128), F32),
        ),
        in_specs=[vmem] * 5,
        out_specs=(vmem, vmem),
        scratch_shapes=[
            pltpu.VMEM((2 * rows, max(sel.shape)), BF16),
            pltpu.VMEM((EXT * rows, 128), F32),
            pltpu.VMEM((ROWS * ROWS, 128), F32),
            pltpu.VMEM((3 * EXT * EXT * 8, 128), F32),
            pltpu.VMEM((2 * EXT * 8, 128), F32),
            pltpu.VMEM((ROWS, 128), F32),
        ],
        compiler_params=pltpu.CompilerParams(vmem_limit_bytes=40 * 1024 * 1024),
        name="smooth",
    )(grid, ends, vectors, eigen, sel)
    return jnp.concatenate([sides[:, :ny, 0:1], out[:, :ny], sides[:, :ny, 1:2]], 2)


def extended_2(cells, sides, width):
    for axis, dim in sides:
        count = lax.axis_size(axis)
        ends = count - 1
        head = lax.slice_in_dim(cells, 0, width, axis=dim)
        tail = lax.slice_in_dim(cells, cells.shape[dim] - width, cells.shape[dim], axis=dim)
        cells = jnp.concatenate(
            [
                lax.ppermute(tail, axis, [(i, (i + 1) % count) for i in range(ends)]),
                cells,
                lax.ppermute(head, axis, [((i + 1) % count, i) for i in range(ends)]),
            ],
            axis=dim,
        )
    return cells


def swapped(array, axis, distance):
    return lax.ppermute(array, axis, [(i, i ^ 1 << distance) for i in range(lax.axis_size(axis))])


def folded_in(value, axis, dim):
    count = lax.axis_size(axis)
    size = value.shape[dim]
    low = lax.slice_in_dim(value, 0, 1, axis=dim)
    high = lax.slice_in_dim(value, size - 1, size, axis=dim)
    below = lax.ppermute(high, axis, [(i, i + 1) for i in range(count - 1)])
    above = lax.ppermute(low, axis, [(i + 1, i) for i in range(count - 1)])
    first = lax.slice_in_dim(value, 1, 2, axis=dim) + below
    last = lax.slice_in_dim(value, size - 2, size - 1, axis=dim) + above
    return jnp.concatenate([first, lax.slice_in_dim(value, 2, size - 2, axis=dim), last], dim)


def on_device(residual, fdm_vectors, fdm_eigen, coarse_basis, x_interior, x_separator):
    cx, cy, cz = residual.shape
    ex, ey, ez = cx // PTS, cy // PTS, cz // PTS
    padded = extended_2(residual, (("gx", 0), ("gy", 1), ("gz", 2)), 1)
    vectors = fdm_vectors.reshape(fdm_vectors.shape[3:])
    eigen = fdm_eigen.reshape(fdm_eigen.shape[3:])
    folded = smooth_call(padded, vectors, eigen, ex, ey, ez)
    for dim, axis in enumerate(("gx", "gy", "gz")):
        folded = folded_in(folded, axis, dim)

    view = (ex // 2, 2, PTS, ey // 2, 2, PTS, ez // 2, 2, PTS)
    weights = coarse_basis[None, None, :, None, None, :, None, None, :]
    coarse_rhs = jnp.sum(residual.reshape(view) * weights, axis=(1, 2, 4, 5, 7, 8)).reshape(-1)
    unknowns = coarse_rhs.shape[0]
    own_factor = x_interior.reshape(unknowns, unknowns)
    levels = x_separator.shape[3]
    sep_factor = x_separator.reshape(levels, unknowns, x_separator.shape[5])
    interior_coef = jnp.dot(coarse_rhs, own_factor, precision=HIGHEST)
    running = jnp.einsum("lvk,v->lk", sep_factor, coarse_rhs, precision=HIGHEST)
    finished = 0
    for axis in ("gz", "gy", "gx"):
        for b in range(lax.axis_size(axis).bit_length() - 1):
            pending = running[finished:]
            running = jnp.concatenate([running[:finished], pending + swapped(pending, axis, b)], 0)
            finished = finished + 1
    coarse_solution = jnp.dot(own_factor, interior_coef, precision=HIGHEST)
    coarse_solution = coarse_solution + jnp.einsum("lvk,lk->v", sep_factor, running, precision=HIGHEST)
    cells = coarse_solution.reshape(ex // 2, 1, 1, ey // 2, 1, 1, ez // 2, 1, 1)
    correction = jnp.broadcast_to(cells * weights, view).reshape(cx, cy, cz)
    return folded + correction


def solution(mesh):
    in_specs = (
        P("gx", "gy", "gz"),
        P("gx", "gy", "gz", None, None, None, None),
        P("gx", "gy", "gz", None, None, None),
        P(),
        P("gx", "gy", "gz", None, None),
        P("gx", "gy", "gz", None, None, None),
    )
    out_specs = P("gx", "gy", "gz")
    return jax.shard_map(
        on_device, mesh=mesh, in_specs=in_specs, out_specs=out_specs, check_vma=False
    )
```

profile of v0, /device:TPU:22, one launch (start us, length us, event | category | flops | bytes accessed | tf_op | source)
XLA Modules:
  0.0 104.8 jit_solution(17109643681171510043)
XLA Ops:
  0.0 1.4 %fusion.14 = (f32[1,16,256]{2,1,0:T(8,128)}, f32[1,16,256]{2,1,0:T(8,128)}) fusion(f32[16,16,256]{2,1,0:T(8,128)} %param.7), kind=kLoop, calls=%fused_computation.53 | loop fusion | bytes 65536 | tf_op jit(solution)/shard_map/slice | solution.py:219
  1.4 2.3 %collective-permute-start = (f32[1,16,256]{2,1,0:T(8,128)}, f32[1,16,256]{2,1,0:T(8,128)}, u32[]{:S(2)}, u32[]{:S(2)}) collective-permute-start(f32[1,16,256]{2,1,0:T(8,128)} %get-tuple-element.20), channel_id=1, source_target_pairs={{0,16},{1,17},{2,18},{3,19},{4,20},{5,21},{6,22},{7,23},{8,24},{9,... | collective-permute-start | bytes 49160 | tf_op jit(solution)/shard_map/ppermute | solution.py:223
  3.7 1.4 %collective-permute-start.1 = (f32[1,16,256]{2,1,0:T(8,128)}, f32[1,16,256]{2,1,0:T(8,128)}, u32[]{:S(2)}, u32[]{:S(2)}) collective-permute-start(f32[1,16,256]{2,1,0:T(8,128)} %get-tuple-element.19), channel_id=1, source_target_pairs={{16,0},{17,1},{18,2},{19,3},{20,4},{21,5},{22,6},{23,7},{24,8},{25... | collective-permute-start | bytes 49160 | tf_op jit(solution)/shard_map/ppermute | solution.py:225
  5.1 4.1 %mul.31 = f32[2,8,2,8,16,2,8]{6,5,4,3,2,1,0:T(2,128)} broadcast(f32[8,8,8]{2,1,0:T(8,128)} %param.10), dimensions={1,3,6} | broadcast | bytes 264192 | tf_op jit(solution)/shard_map/mul | solution.py:260
  9.3 8.0 %mul.32 = f32[16,16,256]{2,1,0:T(8,128)S(1)} reshape(f32[2,8,2,8,16,2,8]{6,5,4,3,2,1,0:T(2,128)} %mul.31) | data formatting | bytes 524288 | tf_op jit(solution)/shard_map/mul | solution.py:260
  17.4 0.0 collective-permute-done
  17.4 0.7 constant_dynamic-update-slice_fusion.2
  18.1 1.0 constant_dynamic-update-slice_fusion.1
  19.1 0.7 copy-done.2
  19.8 0.1 reduce_sum.14
  19.9 0.2 reduce_sum.18
  20.1 0.2 fusion.2
  20.3 0.6 collective-permute-start.12
  20.9 1.3 %constant_dynamic-update-slice_fusion = f32[18,16,256]{2,1,0:T(8,128)} fusion(f32[18,16,256]{2,1,0:T(8,128)} %copy-done.2, f32[1,16,256]{2,1,0:T(8,128)} %collective-permute-done.1), kind=kLoop, calls=%fused_computation.36 | loop fusion | bytes 32768 | tf_op jit(solution)/shard_map/concatenate | solution.py:221
  22.2 1.8 %collective-permute-done.12 = f32[5,256]{1,0:T(8,128)S(1)} collective-permute-done((f32[5,256]{1,0:T(8,128)S(1)}, f32[5,256]{1,0:T(8,128)S(1)}, u32[]{:S(2)}, u32[]{:S(2)}) %collective-permute-start.12) | collective-permute-done | bytes 5152 | tf_op jit(solution)/shard_map/ppermute | solution.py:233
  24.0 0.5 collective-permute-start.13
  24.5 1.0 fusion.13
  25.6 2.1 %collective-permute-done.13 = f32[4,256]{1,0:T(4,128)S(1)} collective-permute-done((f32[4,256]{1,0:T(4,128)S(1)}, f32[4,256]{1,0:T(4,128)S(1)}, u32[]{:S(2)}, u32[]{:S(2)}) %collective-permute-start.13) | collective-permute-done | bytes 4128 | tf_op jit(solution)/shard_map/ppermute | solution.py:233
  27.7 1.6 %collective-permute-start.14 = (f32[3,256]{1,0:T(4,128)S(1)}, f32[3,256]{1,0:T(4,128)S(1)}, u32[]{:S(2)}, u32[]{:S(2)}) collective-permute-start(f32[3,256]{1,0:T(4,128)S(1)} %slice.141), channel_id=1, source_target_pairs={{0,4},{4,0},{8,12},{12,8},{1,5},{5,1},{9,13},{13,9},{2,6},{6,2},{1... | collective-permute-start | bytes 9224 | tf_op jit(solution)/shard_map/ppermute | solution.py:233
  29.3 0.1 convolution_bitcast_fusion.2
  29.4 1.9 %collective-permute-start.3 = (f32[18,1,256]{2,1,0:T(1,128)S(1)}, f32[18,1,256]{2,1,0:T(1,128)S(1)}, u32[]{:S(2)}, u32[]{:S(2)}) collective-permute-start(f32[18,1,256]{2,1,0:T(1,128)S(1)} %get-tuple-element.18), channel_id=1, source_target_pairs={{4,0},{8,4},{12,8},{5,1},{9,5},{13,9},{6,2},{10,6},{14,10},{7,3},{... | collective-permute-start | bytes 55304 | tf_op jit(solution)/shard_map/ppermute | solution.py:225
  31.3 3.9 %collective-permute-start.2 = (f32[18,1,256]{2,1,0:T(1,128)S(1)}, f32[18,1,256]{2,1,0:T(1,128)S(1)}, u32[]{:S(2)}, u32[]{:S(2)}) collective-permute-start(f32[18,1,256]{2,1,0:T(1,128)S(1)} %get-tuple-element.17), channel_id=1, source_target_pairs={{0,4},{4,8},{8,12},{1,5},{5,9},{9,13},{2,6},{6,10},{10,14},{3,7},{... | collective-permute-start | bytes 55304 | tf_op jit(solution)/shard_map/ppermute | solution.py:223
  35.3 0.4 collective-permute-start.15
  35.7 4.1 %collective-permute-done.15 = f32[2,256]{1,0:T(2,128)S(1)} collective-permute-done((f32[2,256]{1,0:T(2,128)S(1)}, f32[2,256]{1,0:T(2,128)S(1)}, u32[]{:S(2)}, u32[]{:S(2)}) %collective-permute-start.15) | collective-permute-done | bytes 2080 | tf_op jit(solution)/shard_map/ppermute | solution.py:233
  39.9 0.1 collective-permute-start.16
  40.0 0.0 collective-permute-done.3
  40.0 0.0 collective-permute-done.2
  40.0 1.0 pad_maximum_fusion.2
  41.0 0.1 fusion.12
  41.1 2.5 %collective-permute-start.5 = (f32[18,18,1]{2,1,0:T(8,128)S(1)}, f32[18,18,1]{2,1,0:T(8,128)S(1)}, u32[]{:S(2)}, u32[]{:S(2)}) collective-permute-start(f32[18,18,1]{2,1,0:T(8,128)S(1)} %get-tuple-element.14), channel_id=1, source_target_pairs={{1,0},{2,1},{3,2},{5,4},{6,5},{7,6},{9,8},{10,9},{11,10},{13,12},{... | collective-permute-start | bytes 3896 | tf_op jit(solution)/shard_map/ppermute | solution.py:225
  43.6 1.3 %collective-permute-start.4 = (f32[18,18,1]{2,1,0:T(8,128)S(1)}, f32[18,18,1]{2,1,0:T(8,128)S(1)}, u32[]{:S(2)}, u32[]{:S(2)}) collective-permute-start(f32[18,18,1]{2,1,0:T(8,128)S(1)} %get-tuple-element.13), channel_id=1, source_target_pairs={{0,1},{1,2},{2,3},{4,5},{5,6},{6,7},{8,9},{9,10},{10,11},{12,13},{... | collective-permute-start | bytes 3896 | tf_op jit(solution)/shard_map/ppermute | solution.py:223
  44.9 0.0 collective-permute-done.16
  45.0 3.9 %collective-permute-done.5 = f32[18,18,1]{2,1,0:T(8,128)S(1)} collective-permute-done((f32[18,18,1]{2,1,0:T(8,128)S(1)}, f32[18,18,1]{2,1,0:T(8,128)S(1)}, u32[]{:S(2)}, u32[]{:S(2)}) %collective-permute-start.5) | collective-permute-done | bytes 1328 | tf_op jit(solution)/shard_map/ppermute | solution.py:225
  48.9 6.6 %collective-permute-done.4 = f32[18,18,1]{2,1,0:T(8,128)S(1)} collective-permute-done((f32[18,18,1]{2,1,0:T(8,128)S(1)}, f32[18,18,1]{2,1,0:T(8,128)S(1)}, u32[]{:S(2)}, u32[]{:S(2)}) %collective-permute-start.4) | collective-permute-done | bytes 1328 | tf_op jit(solution)/shard_map/ppermute | solution.py:223
  55.5 0.1 select_maximum_fusion.ends_in
  55.7 7.2 %smooth.1 = (f32[18,24,256]{2,1,0:T(8,128)S(1)}, f32[18,24,128]{2,1,0:T(8,128)S(1)}) custom-call(f32[18,24,256]{2,1,0:T(8,128)S(1)} %pad.8.grid_in, f32[18,24,128]{2,1,0:T(8,128)S(1)} %select_maximum_fusion.ends_in, bf16[3,10,10,128]{3,2,1,0:T(8,128)(2,1)S(1)} %bitcast.44, f32[3,10,128]{2,1,0:T(8,128)S(1)} %copy.20.eig, bf16[1152,1280]{1,0:T(8,128)(2,1)S(1)} %copy-done.1), custom_call_target="tpu_custom_call" | custom-call | tf_op jit(solution)/shard_map/smooth/pallas_call | solution.py:193
  62.9 0.1 fusion.15
  63.0 0.1 pad_maximum_fusion.5
  63.1 1.6 %collective-permute-start.6 = (f32[1,18,258]{2,1,0:T(8,128)S(1)}, f32[1,18,258]{2,1,0:T(8,128)S(1)}, u32[]{:S(2)}, u32[]{:S(2)}) collective-permute-start(f32[1,18,258]{2,1,0:T(8,128)S(1)} %pad_maximum_fusion.5), channel_id=1, source_target_pairs={{0,16},{1,17},{2,18},{3,19},{4,20},{5,21},{6,22},{7,23},{8,24},{9,... | collective-permute-start | bytes 55736 | tf_op jit(solution)/shard_map/ppermute | solution.py:241
  64.7 0.8 collective-permute-done.6
  65.5 0.1 maximum_add_fusion.2
  65.6 1.3 %collective-permute-start.7 = (f32[1,18,258]{2,1,0:T(8,128)S(1)}, f32[1,18,258]{2,1,0:T(8,128)S(1)}, u32[]{:S(2)}, u32[]{:S(2)}) collective-permute-start(f32[1,18,258]{2,1,0:T(8,128)S(1)} %get-tuple-element.10), channel_id=1, source_target_pairs={{16,0},{17,1},{18,2},{19,3},{20,4},{21,5},{22,6},{23,7},{24,8},{25... | collective-permute-start | bytes 55736 | tf_op jit(solution)/shard_map/ppermute | solution.py:242
  66.9 0.3 pad_maximum_fusion
  67.2 0.0 copy-start.3
  67.3 1.4 %collective-permute-done.7 = f32[1,18,258]{2,1,0:T(8,128)S(1)} collective-permute-done((f32[1,18,258]{2,1,0:T(8,128)S(1)}, f32[1,18,258]{2,1,0:T(8,128)S(1)}, u32[]{:S(2)}, u32[]{:S(2)}) %collective-permute-start.7) | collective-permute-done | bytes 18608 | tf_op jit(solution)/shard_map/ppermute | solution.py:242
  68.7 0.1 maximum_add_fusion.1
  68.9 1.9 %collective-permute-start.8 = (f32[16,1,258]{2,1,0:T(1,128)S(1)}, f32[16,1,258]{2,1,0:T(1,128)S(1)}, u32[]{:S(2)}, u32[]{:S(2)}) collective-permute-start(f32[16,1,258]{2,1,0:T(1,128)S(1)} %pad_maximum_fusion.7), channel_id=1, source_target_pairs={{0,4},{4,8},{8,12},{1,5},{5,9},{9,13},{2,6},{6,10},{10,14},{3,7},{... | collective-permute-start | bytes 49544 | tf_op jit(solution)/shard_map/ppermute | solution.py:241
  70.8 0.2 convolution_bitcast_fusion
  71.0 3.6 %collective-permute-done.8 = f32[16,1,258]{2,1,0:T(1,128)S(1)} collective-permute-done((f32[16,1,258]{2,1,0:T(1,128)S(1)}, f32[16,1,258]{2,1,0:T(1,128)S(1)}, u32[]{:S(2)}, u32[]{:S(2)}) %collective-permute-start.8) | collective-permute-done | bytes 16544 | tf_op jit(solution)/shard_map/ppermute | solution.py:241
  74.6 1.9 %collective-permute-start.9 = (f32[16,1,258]{2,1,0:T(1,128)S(1)}, f32[16,1,258]{2,1,0:T(1,128)S(1)}, u32[]{:S(2)}, u32[]{:S(2)}) collective-permute-start(f32[16,1,258]{2,1,0:T(1,128)S(1)} %get-tuple-element.12), channel_id=1, source_target_pairs={{4,0},{8,4},{12,8},{5,1},{9,5},{13,9},{6,2},{10,6},{14,10},{7,3},{... | collective-permute-start | bytes 49544 | tf_op jit(solution)/shard_map/ppermute | solution.py:242
  76.6 3.7 %collective-permute-done.9 = f32[16,1,258]{2,1,0:T(1,128)S(1)} collective-permute-done((f32[16,1,258]{2,1,0:T(1,128)S(1)}, f32[16,1,258]{2,1,0:T(1,128)S(1)}, u32[]{:S(2)}, u32[]{:S(2)}) %collective-permute-start.9) | collective-permute-done | bytes 16544 | tf_op jit(solution)/shard_map/ppermute | solution.py:242
  80.4 0.1 pad_maximum_fusion.3
  80.5 0.1 slice.135
  80.6 1.3 %collective-permute-start.10 = (f32[16,16,1]{2,1,0:T(8,128)S(1)}, f32[16,16,1]{2,1,0:T(8,128)S(1)}, u32[]{:S(2)}, u32[]{:S(2)}) collective-permute-start(f32[16,16,1]{2,1,0:T(8,128)S(1)} %slice.135), channel_id=1, source_target_pairs={{0,1},{1,2},{2,3},{4,5},{5,6},{6,7},{8,9},{9,10},{10,11},{12,13},{... | collective-permute-start | bytes 3080 | tf_op jit(solution)/shard_map/ppermute | solution.py:241
  81.9 0.1 fusion
  82.0 5.4 %collective-permute-done.10 = f32[16,16,1]{2,1,0:T(8,128)S(1)} collective-permute-done((f32[16,16,1]{2,1,0:T(8,128)S(1)}, f32[16,16,1]{2,1,0:T(8,128)S(1)}, u32[]{:S(2)}, u32[]{:S(2)}) %collective-permute-start.10) | collective-permute-done | bytes 1056 | tf_op jit(solution)/shard_map/ppermute | solution.py:241
  87.4 0.1 slice_add_fusion.1
  87.5 4.1 %collective-permute-start.11 = (f32[16,16,1]{2,1,0:T(8,128)S(1)}, f32[16,16,1]{2,1,0:T(8,128)S(1)}, u32[]{:S(2)}, u32[]{:S(2)}) collective-permute-start(f32[16,16,1]{2,1,0:T(8,128)S(1)} %get-tuple-element.16), channel_id=1, source_target_pairs={{1,0},{2,1},{3,2},{5,4},{6,5},{7,6},{9,8},{10,9},{11,10},{13,12},{... | collective-permute-start | bytes 3080 | tf_op jit(solution)/shard_map/ppermute | solution.py:242
  91.7 0.1 broadcast_multiply_fusion
  91.8 4.1 %broadcast_in_dim.8 = f32[2,8,2,8,16,2,8]{6,5,4,3,2,1,0:T(2,128)} broadcast(f32[8,8,16,8]{3,2,1,0:T(8,128)S(1)} %broadcast_multiply_fusion), dimensions={1,3,4,6} | broadcast | bytes 294912 | tf_op jit(solution)/shard_map/broadcast_in_dim | solution.py:276
  95.9 7.8 %broadcast_in_dim.9 = f32[16,16,256]{2,1,0:T(8,128)S(1)} reshape(f32[2,8,2,8,16,2,8]{6,5,4,3,2,1,0:T(2,128)} %broadcast_in_dim.8) | data formatting | bytes 524288 | tf_op jit(solution)/shard_map/broadcast_in_dim | solution.py:276
  103.7 0.1 slice.136
  103.9 0.0 collective-permute-done.11
  103.9 0.9 maximum_add_fusion
  (38 shorter events, 0.4 us)
Async XLA Ops:
  0.0 20.1 %copy-start = (f32[1,1,1,5,16,256]{5,4,3,2,1,0:T(8,128)S(1)}, f32[1,1,1,5,16,256]{5,4,3,2,1,0:T(8,128)}, u32[]{:S(2)}) copy-start(f32[1,1,1,5,16,256]{5,4,3,2,1,0:T(8,128)} %param.12) | copy-start | bytes 245764
  1.4 16.0 %collective-permute-start = (f32[1,16,256]{2,1,0:T(8,128)}, f32[1,16,256]{2,1,0:T(8,128)}, u32[]{:S(2)}, u32[]{:S(2)}) collective-permute-start(f32[1,16,256]{2,1,0:T(8,128)} %get-tuple-element.20), channel_id=1, source_target_pairs={{0,16},{1,17},{2,18},{3,19},{4,20},{5,21},{6,22},{7,23},{8,24},{9,... | collective-permute-start | bytes 49160 | tf_op jit(solution)/shard_map/ppermute | solution.py:223
  3.7 13.6 %copy-start.4 = (bf16[1,1,1,3,10,10,128]{6,3,5,4,2,1,0:T(4,128)(2,1)S(1)}, bf16[1,1,1,3,10,10,128]{6,3,5,4,2,1,0:T(4,128)(2,1)}, u32[]{:S(2)}) copy-start(bf16[1,1,1,3,10,10,128]{6,3,5,4,2,1,0:T(4,128)(2,1)} %param.8) | copy-start | bytes 230404
  3.7 13.6 %copy-start.6 = (f32[1,1,1,3,10,128]{5,2,4,3,1,0:T(1,128)S(1)}, f32[1,1,1,3,10,128]{5,2,4,3,1,0:T(1,128)}, u32[]{:S(2)}) copy-start(f32[1,1,1,3,10,128]{5,2,4,3,1,0:T(1,128)} %param.9) | copy-start | bytes 46084
  3.7 25.6 %copy-start.5 = (f32[1,1,1,16,16]{4,3,2,1,0:T(8,128)S(1)}, f32[1,1,1,16,16]{4,3,2,1,0:T(8,128)}, u32[]{:S(2)}) copy-start(f32[1,1,1,16,16]{4,3,2,1,0:T(8,128)} %param.11) | copy-start | bytes 3076
  3.7 17.2 %collective-permute-start.1 = (f32[1,16,256]{2,1,0:T(8,128)}, f32[1,16,256]{2,1,0:T(8,128)}, u32[]{:S(2)}, u32[]{:S(2)}) collective-permute-start(f32[1,16,256]{2,1,0:T(8,128)} %get-tuple-element.19), channel_id=1, source_target_pairs={{16,0},{17,1},{18,2},{19,3},{20,4},{21,5},{22,6},{23,7},{24,8},{25... | collective-permute-start | bytes 49160 | tf_op jit(solution)/shard_map/ppermute | solution.py:225
  9.3 46.4 %copy-start.1 = (bf16[1152,1280]{1,0:T(8,128)(2,1)S(1)}, bf16[1152,1280]{1,0:T(8,128)(2,1)}, u32[]{:S(2)}) copy-start(bf16[1152,1280]{1,0:T(8,128)(2,1)} %constant.6.clone.sel) | copy-start | bytes 8847364
  19.1 0.7 copy-start.2
  20.3 3.7 %collective-permute-start.12 = (f32[5,256]{1,0:T(8,128)S(1)}, f32[5,256]{1,0:T(8,128)S(1)}, u32[]{:S(2)}, u32[]{:S(2)}) collective-permute-start(f32[5,256]{1,0:T(8,128)S(1)} %bitcast.46), channel_id=1, source_target_pairs={{0,1},{1,0},{2,3},{3,2},{4,5},{5,4},{6,7},{7,6},{8,9},{9,8},{10,11... | collective-permute-start | bytes 15368 | tf_op jit(solution)/shard_map/ppermute | solution.py:233
  24.0 3.6 %collective-permute-start.13 = (f32[4,256]{1,0:T(4,128)S(1)}, f32[4,256]{1,0:T(4,128)S(1)}, u32[]{:S(2)}, u32[]{:S(2)}) collective-permute-start(f32[4,256]{1,0:T(4,128)S(1)} %slice.140), channel_id=1, source_target_pairs={{0,2},{1,3},{2,0},{3,1},{4,6},{5,7},{6,4},{7,5},{8,10},{9,11},{10,... | collective-permute-start | bytes 12296 | tf_op jit(solution)/shard_map/ppermute | solution.py:233
  27.7 7.6 %collective-permute-start.14 = (f32[3,256]{1,0:T(4,128)S(1)}, f32[3,256]{1,0:T(4,128)S(1)}, u32[]{:S(2)}, u32[]{:S(2)}) collective-permute-start(f32[3,256]{1,0:T(4,128)S(1)} %slice.141), channel_id=1, source_target_pairs={{0,4},{4,0},{8,12},{12,8},{1,5},{5,1},{9,13},{13,9},{2,6},{6,2},{1... | collective-permute-start | bytes 9224 | tf_op jit(solution)/shard_map/ppermute | solution.py:233
  29.4 10.5 %collective-permute-start.3 = (f32[18,1,256]{2,1,0:T(1,128)S(1)}, f32[18,1,256]{2,1,0:T(1,128)S(1)}, u32[]{:S(2)}, u32[]{:S(2)}) collective-permute-start(f32[18,1,256]{2,1,0:T(1,128)S(1)} %get-tuple-element.18), channel_id=1, source_target_pairs={{4,0},{8,4},{12,8},{5,1},{9,5},{13,9},{6,2},{10,6},{14,10},{7,3},{... | collective-permute-start | bytes 55304 | tf_op jit(solution)/shard_map/ppermute | solution.py:225
  31.3 8.6 %collective-permute-start.2 = (f32[18,1,256]{2,1,0:T(1,128)S(1)}, f32[18,1,256]{2,1,0:T(1,128)S(1)}, u32[]{:S(2)}, u32[]{:S(2)}) collective-permute-start(f32[18,1,256]{2,1,0:T(1,128)S(1)} %get-tuple-element.17), channel_id=1, source_target_pairs={{0,4},{4,8},{8,12},{1,5},{5,9},{9,13},{2,6},{6,10},{10,14},{3,7},{... | collective-permute-start | bytes 55304 | tf_op jit(solution)/shard_map/ppermute | solution.py:223
  35.3 4.5 %collective-permute-start.15 = (f32[2,256]{1,0:T(2,128)S(1)}, f32[2,256]{1,0:T(2,128)S(1)}, u32[]{:S(2)}, u32[]{:S(2)}) collective-permute-start(f32[2,256]{1,0:T(2,128)S(1)} %slice.142), channel_id=1, source_target_pairs={{0,8},{4,12},{8,0},{12,4},{1,9},{5,13},{9,1},{13,5},{2,10},{6,14},... | collective-permute-start | bytes 6152 | tf_op jit(solution)/shard_map/ppermute | solution.py:233
  39.9 5.0 %collective-permute-start.16 = (f32[1,256]{1,0:T(1,128)S(1)}, f32[1,256]{1,0:T(1,128)S(1)}, u32[]{:S(2)}, u32[]{:S(2)}) collective-permute-start(f32[1,256]{1,0:T(1,128)S(1)} %slice.143), channel_id=1, source_target_pairs={{0,16},{16,0},{1,17},{17,1},{2,18},{18,2},{3,19},{19,3},{4,20},{20... | collective-permute-start | bytes 3080 | tf_op jit(solution)/shard_map/ppermute | solution.py:233
  41.1 7.8 %collective-permute-start.5 = (f32[18,18,1]{2,1,0:T(8,128)S(1)}, f32[18,18,1]{2,1,0:T(8,128)S(1)}, u32[]{:S(2)}, u32[]{:S(2)}) collective-permute-start(f32[18,18,1]{2,1,0:T(8,128)S(1)} %get-tuple-element.14), channel_id=1, source_target_pairs={{1,0},{2,1},{3,2},{5,4},{6,5},{7,6},{9,8},{10,9},{11,10},{13,12},{... | collective-permute-start | bytes 3896 | tf_op jit(solution)/shard_map/ppermute | solution.py:225
  43.6 11.9 %collective-permute-start.4 = (f32[18,18,1]{2,1,0:T(8,128)S(1)}, f32[18,18,1]{2,1,0:T(8,128)S(1)}, u32[]{:S(2)}, u32[]{:S(2)}) collective-permute-start(f32[18,18,1]{2,1,0:T(8,128)S(1)} %get-tuple-element.13), channel_id=1, source_target_pairs={{0,1},{1,2},{2,3},{4,5},{5,6},{6,7},{8,9},{9,10},{10,11},{12,13},{... | collective-permute-start | bytes 3896 | tf_op jit(solution)/shard_map/ppermute | solution.py:223
  63.1 2.5 %collective-permute-start.6 = (f32[1,18,258]{2,1,0:T(8,128)S(1)}, f32[1,18,258]{2,1,0:T(8,128)S(1)}, u32[]{:S(2)}, u32[]{:S(2)}) collective-permute-start(f32[1,18,258]{2,1,0:T(8,128)S(1)} %pad_maximum_fusion.5), channel_id=1, source_target_pairs={{0,16},{1,17},{2,18},{3,19},{4,20},{5,21},{6,22},{7,23},{8,24},{9,... | collective-permute-start | bytes 55736 | tf_op jit(solution)/shard_map/ppermute | solution.py:241
  65.6 3.1 %collective-permute-start.7 = (f32[1,18,258]{2,1,0:T(8,128)S(1)}, f32[1,18,258]{2,1,0:T(8,128)S(1)}, u32[]{:S(2)}, u32[]{:S(2)}) collective-permute-start(f32[1,18,258]{2,1,0:T(8,128)S(1)} %get-tuple-element.10), channel_id=1, source_target_pairs={{16,0},{17,1},{18,2},{19,3},{20,4},{21,5},{22,6},{23,7},{24,8},{25... | collective-permute-start | bytes 55736 | tf_op jit(solution)/shard_map/ppermute | solution.py:242
  67.2 24.4 %copy-start.3 = (f32[8,8,8]{2,1,0:T(8,128)S(1)}, f32[8,8,8]{2,1,0:T(8,128)}, u32[]{:S(2)}) copy-start(f32[8,8,8]{2,1,0:T(8,128)} %param.10) | copy-start | bytes 6148
  68.9 5.7 %collective-permute-start.8 = (f32[16,1,258]{2,1,0:T(1,128)S(1)}, f32[16,1,258]{2,1,0:T(1,128)S(1)}, u32[]{:S(2)}, u32[]{:S(2)}) collective-permute-start(f32[16,1,258]{2,1,0:T(1,128)S(1)} %pad_maximum_fusion.7), channel_id=1, source_target_pairs={{0,4},{4,8},{8,12},{1,5},{5,9},{9,13},{2,6},{6,10},{10,14},{3,7},{... | collective-permute-start | bytes 49544 | tf_op jit(solution)/shard_map/ppermute | solution.py:241
  74.6 5.7 %collective-permute-start.9 = (f32[16,1,258]{2,1,0:T(1,128)S(1)}, f32[16,1,258]{2,1,0:T(1,128)S(1)}, u32[]{:S(2)}, u32[]{:S(2)}) collective-permute-start(f32[16,1,258]{2,1,0:T(1,128)S(1)} %get-tuple-element.12), channel_id=1, source_target_pairs={{4,0},{8,4},{12,8},{5,1},{9,5},{13,9},{6,2},{10,6},{14,10},{7,3},{... | collective-permute-start | bytes 49544 | tf_op jit(solution)/shard_map/ppermute | solution.py:242
  80.6 6.9 %collective-permute-start.10 = (f32[16,16,1]{2,1,0:T(8,128)S(1)}, f32[16,16,1]{2,1,0:T(8,128)S(1)}, u32[]{:S(2)}, u32[]{:S(2)}) collective-permute-start(f32[16,16,1]{2,1,0:T(8,128)S(1)} %slice.135), channel_id=1, source_target_pairs={{0,1},{1,2},{2,3},{4,5},{5,6},{6,7},{8,9},{9,10},{10,11},{12,13},{... | collective-permute-start | bytes 3080 | tf_op jit(solution)/shard_map/ppermute | solution.py:241
  87.5 16.3 %collective-permute-start.11 = (f32[16,16,1]{2,1,0:T(8,128)S(1)}, f32[16,16,1]{2,1,0:T(8,128)S(1)}, u32[]{:S(2)}, u32[]{:S(2)}) collective-permute-start(f32[16,16,1]{2,1,0:T(8,128)S(1)} %get-tuple-element.16), channel_id=1, source_target_pairs={{1,0},{2,1},{3,2},{5,4},{6,5},{7,6},{9,8},{10,9},{11,10},{13,12},{... | collective-permute-start | bytes 3080 | tf_op jit(solution)/shard_map/ppermute | solution.py:242
where the time goes:
time: 105 us
  waiting for transfers between devices  33.6 us (32%)
  local copies, waits for them, and re-layouts  29.9 us (28%)
  starting transfers between devices  28.7 us (27%)
  Pallas kernels  7.2 us (7%)
  other arithmetic  4.3 us (4%)
    mul x2, local copies, waits for them, and re-layouts, on_device(): residual.reshape(view) * weights  12.1 us
    broadcast_in_dim x2, local copies, waits for them, and re-layouts, on_device(): correction = jnp.broadcast_to(cells * weights, view).reshape(cx, cy, cz)  11.9 us
    ppermute x3, waiting for transfers between devices, folded_in(): below = lax.ppermute(high, axis, [(i, i + 1) for i in range(count - 1)])  9.88 us
    ppermute x5, waiting for transfers between devices, swapped(): lax.ppermute(array, axis, [(i, i ^ 1 << distance) for i in range(lax.axis...  8.02 us
    ppermute x3, starting transfers between devices, extended_2(): lax.ppermute(tail, axis, [(i, (i + 1) % count) for i in range(ends)])  7.54 us
    ppermute x3, starting transfers between devices, folded_in(): above = lax.ppermute(low, axis, [(i + 1, i) for i in range(count - 1)])  7.31 us
    pallas_call x1, Pallas kernels, smooth_call(): pl.pallas_call(functools.partial(smooth_kernel, ex, ey), out_shape=(jax.S...  7.2 us
    ppermute x3, waiting for transfers between devices, extended_2(): lax.ppermute(tail, axis, [(i, (i + 1) % count) for i in range(ends)])  6.63 us
  transfers between devices with their start and end apart: 17, of which 10 were waited for; matrix products, arithmetic and copies ran while one was open for 30% of the time, Pallas kernels for 0%

commit v1 on v0

--- a/solution.py
+++ b/solution.py
@@ -11,7 +11,6 @@
 PTS = 8
 EXT = PTS + 2
 ROWS = 16
-HIGHEST = lax.Precision.HIGHEST
 F32 = jnp.float32
 BF16 = jnp.bfloat16
 
@@ -170,7 +169,9 @@
         ends_ref[x : x + EXT, y : y + EXT, :] += side[:, 0:EXT]
 
 
-def smooth_kernel(ex, ey, grid_in, ends_in, vec, eig, sel, grid_out, ends_out, parts, buf, turn, modes, lam, lamx):
+def smooth_kernel(ex, ey, grid_in, ends_in, vec, eig, sel, out, parts, buf, turn, modes, lam, lamx):
+    size = grid_in.shape[2]
+    grid_out, ends_out = out.at[:, :, 0:size], out.at[:, :, size : size + 128]
     turn[...] = jnp.zeros_like(turn)
     prepare_modes(vec, eig, modes, lam, lamx)
     gather_elements(grid_in, ends_in, sel, parts, buf, ex, ey)
@@ -180,24 +181,16 @@
     scatter_elements(buf, sel, parts, grid_out, ends_out, ex, ey)
 
 
-def smooth_call(padded, vectors, eigen, ex, ey, ez):
-    nx, ny, nz = padded.shape
-    size = nz - 2
-    tall = PTS * (ey - 1) + ROWS
+def smooth_call(grid, ends, vectors, eigen, ex, ey, ez):
+    nx, tall, size = grid.shape
     sel = jnp.asarray(selection(ex * ey, ez), BF16)
-    grid = jnp.pad(padded[:, :, 1:-1], ((0, 0), (0, tall - ny), (0, 0)))
-    ends = jnp.stack([padded[:, :, 0], padded[:, :, -1]], -1)
-    ends = jnp.pad(ends, ((0, 0), (0, tall - ny), (0, 126)))
     vmem = pl.BlockSpec(memory_space=pltpu.VMEM)
     rows = EXT * ROWS
-    out, sides = pl.pallas_call(
+    return pl.pallas_call(
         functools.partial(smooth_kernel, ex, ey),
-        out_shape=(
-            jax.ShapeDtypeStruct((nx, tall, size), F32),
-            jax.ShapeDtypeStruct((nx, tall, 128), F32),
-        ),
+        out_shape=jax.ShapeDtypeStruct((nx, tall, size + 128), F32),
         in_specs=[vmem] * 5,
-        out_specs=(vmem, vmem),
+        out_specs=vmem,
         scratch_shapes=[
             pltpu.VMEM((2 * rows, max(sel.shape)), BF16),
             pltpu.VMEM((EXT * rows, 128), F32),
@@ -209,72 +202,293 @@
         compiler_params=pltpu.CompilerParams(vmem_limit_bytes=40 * 1024 * 1024),
         name="smooth",
     )(grid, ends, vectors, eigen, sel)
-    return jnp.concatenate([sides[:, :ny, 0:1], out[:, :ny], sides[:, :ny, 1:2]], 2)
-
-
-def extended_2(cells, sides, width):
-    for axis, dim in sides:
-        count = lax.axis_size(axis)
-        ends = count - 1
-        head = lax.slice_in_dim(cells, 0, width, axis=dim)
-        tail = lax.slice_in_dim(cells, cells.shape[dim] - width, cells.shape[dim], axis=dim)
-        cells = jnp.concatenate(
-            [
-                lax.ppermute(tail, axis, [(i, (i + 1) % count) for i in range(ends)]),
-                cells,
-                lax.ppermute(head, axis, [((i + 1) % count, i) for i in range(ends)]),
-            ],
-            axis=dim,
+
+
+AXES = ("gx", "gy", "gz")
+MESH = pl.DeviceIdType.MESH
+
+
+def tree_bits(sizes):
+    return [(a, 1 << b) for a in (2, 1, 0) for b in range(sizes[a].bit_length() - 1)]
+
+
+def greet(sizes, here, bits):
+    barrier = pltpu.get_barrier_semaphore()
+    for a in range(3):
+        for step in (-1, 1):
+            @pl.when((here[a] + step >= 0) & (here[a] + step < sizes[a]))
+            def _(a=a, step=step):
+                pl.semaphore_signal(barrier, inc=1, device_id={AXES[a]: here[a] + step}, device_id_type=MESH)
+    for a, bit in bits:
+        pl.semaphore_signal(barrier, inc=1, device_id={AXES[a]: partner(here[a], bit)}, device_id_type=MESH)
+    peers = len(bits)
+    for a in range(3):
+        peers = peers + jnp.where(here[a] > 0, 1, 0) + jnp.where(here[a] < sizes[a] - 1, 1, 0)
+    pl.semaphore_wait(barrier, peers)
+
+
+def partner(index, bit):
+    return index + bit * (1 - 2 * ((index // bit) % 2))
+
+
+class Sides:
+    def __init__(self, a, sizes, here, low, high, slots, sent, came):
+        self.below, self.above = here[a] > 0, here[a] < sizes[a] - 1
+        self.down = pltpu.make_async_remote_copy(
+            low, slots.at[1], sent.at[2 * a], came.at[2 * a + 1],
+            device_id={AXES[a]: here[a] - 1}, device_id_type=MESH,
         )
-    return cells
-
-
-def swapped(array, axis, distance):
-    return lax.ppermute(array, axis, [(i, i ^ 1 << distance) for i in range(lax.axis_size(axis))])
-
-
-def folded_in(value, axis, dim):
-    count = lax.axis_size(axis)
-    size = value.shape[dim]
-    low = lax.slice_in_dim(value, 0, 1, axis=dim)
-    high = lax.slice_in_dim(value, size - 1, size, axis=dim)
-    below = lax.ppermute(high, axis, [(i, i + 1) for i in range(count - 1)])
-    above = lax.ppermute(low, axis, [(i + 1, i) for i in range(count - 1)])
-    first = lax.slice_in_dim(value, 1, 2, axis=dim) + below
-    last = lax.slice_in_dim(value, size - 2, size - 1, axis=dim) + above
-    return jnp.concatenate([first, lax.slice_in_dim(value, 2, size - 2, axis=dim), last], dim)
+        self.up = pltpu.make_async_remote_copy(
+            high, slots.at[0], sent.at[2 * a + 1], came.at[2 * a],
+            device_id={AXES[a]: here[a] + 1}, device_id_type=MESH,
+        )
+
+    def start(self):
+        pl.when(self.below)(self.down.start)
+        pl.when(self.above)(self.up.start)
+
+    def arrive(self):
+        pl.when(self.below)(self.up.wait_recv)
+        pl.when(self.above)(self.down.wait_recv)
+
+    def finish(self):
+        pl.when(self.below)(self.down.wait_send)
+        pl.when(self.above)(self.up.wait_send)
+
+
+class Tree:
+    def __init__(self, bits, first, here, slots, inbox, sent, came):
+        self.first, self.slots, self.inbox = first, slots, inbox
+        self.copies = [
+            pltpu.make_async_remote_copy(
+                slots.at[n], inbox.at[n], sent.at[n], came.at[n],
+                device_id={AXES[a]: partner(here[a], bit)}, device_id_type=MESH,
+            )
+            for n, (a, bit) in enumerate(bits)
+        ]
+
+    def start(self, n):
+        if n < len(self.copies):
+            self.copies[n].start()
+
+    def step(self, n):
+        if n < len(self.copies):
+            self.copies[n].wait_recv()
+            level = lax.broadcasted_iota(jnp.int32, self.slots.shape[1:], 0)
+            self.slots[n + 1] = self.slots[n] + jnp.where(level >= self.first + n, self.inbox[n], 0.0)
+
+    def finish(self):
+        for copy in self.copies:
+            copy.wait_send()
+
+
+def place():
+    return [lax.axis_index(axis) for axis in AXES]
+
+
+def halo_kernel(sizes, bits, res, basis, own, sep, grid, ends, run, base, xin, yout, yin, zout, zin, slots, inbox,
+                sent, came, tree_sent, tree_came):
+    cx, cy, size = res.shape
+    nx, tall = cx + 2, grid.shape[1]
+    here = place()
+    for ref in (xin, yin, zin, grid, slots, yout):
+        ref[...] = jnp.zeros_like(ref)
+    greet(sizes, here, bits)
+    along_x = Sides(0, sizes, here, res.at[0], res.at[cx - 1], xin, sent, came)
+    along_x.start()
+
+    span = 2 * PTS
+    weighted = jnp.zeros((PTS, size), F32)
+    for x in range(cx):
+        for y in range(0, cy, PTS):
+            weighted = weighted + res[x, y : y + PTS, :] * basis[x % PTS]
+    unknowns = own.shape[0]
+    line = jnp.sum(weighted, axis=0, keepdims=True)
+    inside = lax.broadcasted_iota(jnp.int32, (unknowns, size), 1) // span == lax.broadcasted_iota(
+        jnp.int32, (unknowns, size), 0
+    )
+    rhs = jnp.sum(jnp.where(inside, line, 0.0), axis=1, keepdims=True)
+    for l in range(sep.shape[0]):
+        slots[0, l : l + 1, :] = jnp.sum(sep[l] * rhs, axis=0, keepdims=True)
+    tree = Tree(bits, 0, here, slots, inbox, tree_sent, tree_came)
+    tree.start(0)
+    coef = jnp.sum(own[...] * rhs, axis=0, keepdims=True)
+    base[...] = jnp.broadcast_to(jnp.sum(own[...] * coef, axis=1, keepdims=True), base.shape)
+    for x in range(cx):
+        grid[x + 1, 1 : cy + 1, :] = res[x]
+
+    along_x.arrive()
+    grid[0, 1 : cy + 1, :] = xin[0]
+    grid[nx - 1, 1 : cy + 1, :] = xin[1]
+    for x in range(nx):
+        yout[0, x : x + 1, :] = grid[x, 1:2, :]
+        yout[1, x : x + 1, :] = grid[x, cy : cy + 1, :]
+    along_y = Sides(1, sizes, here, yout.at[0], yout.at[1], yin, sent, came)
+    along_y.start()
+    tree.step(0)
+    tree.start(1)
+    along_y.arrive()
+    for x in range(nx):
+        grid[x, 0:1, :] = yin[0, x : x + 1, :]
+        grid[x, cy + 1 : cy + 2, :] = yin[1, x : x + 1, :]
+
+    lane = lax.broadcasted_iota(jnp.int32, (1, 128), 1)
+    rows = nx * tall
+    padded = zout.shape[2]
+    flat = grid[...].reshape(rows, size)
+    both = jnp.where(lane == 0, flat[:, 0:128], flat[:, size - 128 : size])
+    both = jnp.concatenate([both, jnp.zeros((padded - rows, 128), F32)], 0)
+    turned = both.T
+    zout[0] = turned[0:8]
+    zout[1] = turned[120:128]
+    along_z = Sides(2, sizes, here, zout.at[0], zout.at[1], zin, sent, came)
+    along_z.start()
+    tree.step(1)
+    tree.start(2)
+    along_z.arrive()
+    row = lax.broadcasted_iota(jnp.int32, (8, padded), 0)
+    head = jnp.where(row == 0, zin[0, 7:8, :], jnp.where(row == 1, zin[1, 0:1, :], 0.0))
+    turned = jnp.concatenate([head, jnp.zeros((120, padded), F32)], 0).T
+    ends[...] = turned[0:rows].reshape(nx, tall, 128)
+    for n in range(2, len(bits)):
+        tree.step(n)
+        tree.start(n + 1)
+    run[...] = slots[len(bits)]
+    for sides in (along_x, along_y, along_z):
+        sides.finish()
+    tree.finish()
+
+
+def fold_kernel(sizes, bits, first, fold, basis, sep, run, base, out, acc, xin, yout, yin, zout, zin, slots, inbox,
+                sent, came, tree_sent, tree_came):
+    cx, cy, size = out.shape
+    nx, tall = cx + 2, fold.shape[1]
+    here = place()
+    for ref in (xin, yin, zin):
+        ref[...] = jnp.zeros_like(ref)
+    slots[0] = run[...]
+    greet(sizes, here, bits)
+    along_x = Sides(0, sizes, here, fold.at[0], fold.at[nx - 1], xin, sent, came)
+    along_x.start()
+    tree = Tree(bits, first, here, slots, inbox, tree_sent, tree_came)
+    tree.start(0)
+    acc[...] = fold[1 : nx - 1]
+    along_x.arrive()
+    acc[0] += xin[0]
+    acc[cx - 1] += xin[1]
+    for x in range(cx):
+        yout[0, x : x + 1, :] = acc[x, 0:1, :]
+        yout[1, x : x + 1, :] = acc[x, cy + 1 : cy + 2, :]
+    along_y = Sides(1, sizes, here, yout.at[0], yout.at[1], yin, sent, came)
+    along_y.start()
+    tree.step(0)
+    tree.start(1)
+    along_y.arrive()
+    for x in range(cx):
+        acc[x, 1:2, :] += yin[0, x : x + 1, :]
+        acc[x, cy : cy + 1, :] += yin[1, x : x + 1, :]
+    turned = acc[:, :, size : size + 128].reshape(cx * tall, 128).T
+    zout[...] = turned[0:8]
+    along_z = Sides(2, sizes, here, zout, zout, zin, sent, came)
+    along_z.start()
+    for n in range(1, len(bits)):
+        tree.step(n)
+        tree.start(n + 1)
+    last = slots[len(bits)]
+    answer = base[:, 0:1]
+    for l in range(sep.shape[0]):
+        answer = answer + jnp.sum(sep[l] * last[l : l + 1], axis=1, keepdims=True)
+    unknowns = answer.shape[0]
+    inside = lax.broadcasted_iota(jnp.int32, (unknowns, size), 1) // (2 * PTS) == lax.broadcasted_iota(
+        jnp.int32, (unknowns, size), 0
+    )
+    line = jnp.sum(jnp.where(inside, answer, 0.0), axis=0, keepdims=True)
+    for x in range(cx):
+        bump = basis[x % PTS] * line
+        for y in range(0, cy, PTS):
+            out[x, y : y + PTS, :] = acc[x, y + 1 : y + 1 + PTS, 0:size] + bump
+    along_z.arrive()
+    padded = cx * tall
+    row = lax.broadcasted_iota(jnp.int32, (8, padded), 0)
+    low = jnp.where(row == 0, zin[0, 1:2, :], 0.0)
+    high = jnp.where(row == 7, zin[1, 0:1, :], 0.0)
+    turned = jnp.concatenate([low, jnp.zeros((112, padded), F32), high], 0).T.reshape(cx, tall, 128)
+    lane = lax.broadcasted_iota(jnp.int32, (1, 128), 1)
+    extra = turned[:, 1 : cy + 1]
+    out[:, :, 0:128] += jnp.where(lane < 64, extra, 0.0)
+    out[:, :, size - 128 : size] += jnp.where(lane >= 64, extra, 0.0)
+    for sides in (along_x, along_y, along_z):
+        sides.finish()
+    tree.finish()
 
 
 def on_device(residual, fdm_vectors, fdm_eigen, coarse_basis, x_interior, x_separator):
     cx, cy, cz = residual.shape
     ex, ey, ez = cx // PTS, cy // PTS, cz // PTS
-    padded = extended_2(residual, (("gx", 0), ("gy", 1), ("gz", 2)), 1)
+    sizes = [lax.axis_size(axis) for axis in AXES]
     vectors = fdm_vectors.reshape(fdm_vectors.shape[3:])
     eigen = fdm_eigen.reshape(fdm_eigen.shape[3:])
-    folded = smooth_call(padded, vectors, eigen, ex, ey, ez)
-    for dim, axis in enumerate(("gx", "gy", "gz")):
-        folded = folded_in(folded, axis, dim)
-
-    view = (ex // 2, 2, PTS, ey // 2, 2, PTS, ez // 2, 2, PTS)
-    weights = coarse_basis[None, None, :, None, None, :, None, None, :]
-    coarse_rhs = jnp.sum(residual.reshape(view) * weights, axis=(1, 2, 4, 5, 7, 8)).reshape(-1)
-    unknowns = coarse_rhs.shape[0]
-    own_factor = x_interior.reshape(unknowns, unknowns)
-    levels = x_separator.shape[3]
-    sep_factor = x_separator.reshape(levels, unknowns, x_separator.shape[5])
-    interior_coef = jnp.dot(coarse_rhs, own_factor, precision=HIGHEST)
-    running = jnp.einsum("lvk,v->lk", sep_factor, coarse_rhs, precision=HIGHEST)
-    finished = 0
-    for axis in ("gz", "gy", "gx"):
-        for b in range(lax.axis_size(axis).bit_length() - 1):
-            pending = running[finished:]
-            running = jnp.concatenate([running[:finished], pending + swapped(pending, axis, b)], 0)
-            finished = finished + 1
-    coarse_solution = jnp.dot(own_factor, interior_coef, precision=HIGHEST)
-    coarse_solution = coarse_solution + jnp.einsum("lvk,lk->v", sep_factor, running, precision=HIGHEST)
-    cells = coarse_solution.reshape(ex // 2, 1, 1, ey // 2, 1, 1, ez // 2, 1, 1)
-    correction = jnp.broadcast_to(cells * weights, view).reshape(cx, cy, cz)
-    return folded + correction
+    own = x_interior.reshape(x_interior.shape[3:])
+    sep = x_separator.reshape(x_separator.shape[3:])
+    levels, unknowns, width = sep.shape
+    basis = jnp.tile(coarse_basis, (1, 1, ez))
+    bits = tree_bits(sizes)
+    early = bits[:3]
+    late = bits[3:]
+    nx, tall = cx + 2, PTS * (ey - 1) + ROWS
+    deep = -(-levels // 8) * 8
+    wide = -(-(nx * tall) // 128) * 128
+    flat = -(-nx // 8) * 8
+    vmem = pl.BlockSpec(memory_space=pltpu.VMEM)
+    dma = pltpu.SemaphoreType.DMA
+
+    def tree_scratch(rounds):
+        return [pltpu.VMEM((rounds + 1, deep, width), F32), pltpu.VMEM((max(rounds, 1), deep, width), F32)]
+
+    def semaphores(rounds):
+        return [dma((6,)), dma((6,)), dma((max(rounds, 1),)), dma((max(rounds, 1),))]
+
+    grid, ends, run, base = pl.pallas_call(
+        functools.partial(halo_kernel, sizes, early),
+        out_shape=(
+            jax.ShapeDtypeStruct((nx, tall, cz), F32),
+            jax.ShapeDtypeStruct((nx, tall, 128), F32),
+            jax.ShapeDtypeStruct((deep, width), F32),
+            jax.ShapeDtypeStruct((unknowns, 128), F32),
+        ),
+        in_specs=[vmem] * 4,
+        out_specs=(vmem,) * 4,
+        scratch_shapes=[
+            pltpu.VMEM((2, cy, cz), F32),
+            pltpu.VMEM((2, flat, cz), F32),
+            pltpu.VMEM((2, flat, cz), F32),
+            pltpu.VMEM((2, 8, wide), F32),
+            pltpu.VMEM((2, 8, wide), F32),
+        ] + tree_scratch(len(early)) + semaphores(len(early)),
+        compiler_params=pltpu.CompilerParams(
+            collective_id=0, has_side_effects=True, vmem_limit_bytes=32 * 1024 * 1024
+        ),
+        name="halo",
+    )(residual, basis, own, sep)
+    folded = smooth_call(grid, ends, vectors, eigen, ex, ey, ez)
+    return pl.pallas_call(
+        functools.partial(fold_kernel, sizes, late, len(early)),
+        out_shape=jax.ShapeDtypeStruct((cx, cy, cz), F32),
+        in_specs=[vmem] * 5,
+        out_specs=vmem,
+        scratch_shapes=[
+            pltpu.VMEM((cx, tall, cz + 128), F32),
+            pltpu.VMEM((2, tall, cz + 128), F32),
+            pltpu.VMEM((2, cx, cz + 128), F32),
+            pltpu.VMEM((2, cx, cz + 128), F32),
+            pltpu.VMEM((8, cx * tall), F32),
+            pltpu.VMEM((2, 8, cx * tall), F32),
+        ] + tree_scratch(len(late)) + semaphores(len(late)),
+        compiler_params=pltpu.CompilerParams(
+            collective_id=1, has_side_effects=True, vmem_limit_bytes=32 * 1024 * 1024
+        ),
+        name="fold",
+    )(folded, basis, sep, run, base)
 
 
 def solution(mesh):

time: 105 us -> 37.1 us (0.35)
  the two profiles are of different devices: /device:TPU:22 before, /device:TPU:0 now
where the time goes in v1:
time: 37.1 us; the launch traced here: 36.7 us
  Pallas kernels  28.6 us (77%)
  local copies, waits for them, and re-layouts  8.08 us (22%)
    pallas_call x1, Pallas kernels, on_device(): pl.pallas_call(functools.partial(halo_kernel, sizes, early), out_shape=(j...  12.9 us
    pallas_call x1, Pallas kernels, on_device(): pl.pallas_call(functools.partial(fold_kernel, sizes, late, len(early)), o...  8.5 us
    pallas_call x1, Pallas kernels, smooth_call(): pl.pallas_call(functools.partial(smooth_kernel, ex, ey), out_shape=jax.Sh...  7.25 us
    unnamed x13, local copies, waits for them, and re-layouts  6.71 us
    another operation x2, local copies, waits for them, and re-layouts, on_device(): basis = jnp.tile(coarse_basis, (1, 1, ez))  1.36 us

profile of v1, /device:TPU:0, one launch (start us, length us, event | category | flops | bytes accessed | tf_op | source)
XLA Modules:
  0.0 36.7 jit_solution(16674747571771339012)
XLA Ops:
  0.0 0.7 %copy.15 = f32[1,1,1,3,10,128]{5,3,4,2,1,0:T(4,128)S(1)} copy(f32[1,1,1,3,10,128]{5,2,4,3,1,0:T(1,128)} %param.9) | data formatting | bytes 30720 | tf_op args[2]
  0.7 0.9 %copy.14 = bf16[1,1,1,3,10,10,128]{6,5,4,3,2,1,0:T(8,128)(2,1)S(1)} copy(bf16[1,1,1,3,10,10,128]{6,3,5,4,2,1,0:T(4,128)(2,1)} %param.8) | data formatting | bytes 153600 | tf_op args[1]
  1.7 0.8 %tile.4 = f32[8,8,32,8]{3,2,1,0:T(8,128)S(1)} broadcast(f32[8,8,8]{2,1,0:T(8,128)} %param.10), dimensions={0,1,3} | broadcast | bytes 67584 | tf_op jit(solution)/shard_map/tile | solution.py:434
  2.5 0.0 copy-start.2
  2.5 0.5 %tile.10.basis = f32[8,8,256]{2,1,0:T(8,128)S(1)} reshape(f32[8,8,32,8]{3,2,1,0:T(8,128)S(1)} %tile.4) | data formatting | bytes 131072 | tf_op jit(solution)/shard_map/tile | solution.py:434
  3.0 0.0 copy-start.1
  3.0 0.9 %copy-done.1 = f32[1,1,1,5,16,256]{5,4,3,2,1,0:T(8,128)S(1)} copy-done((f32[1,1,1,5,16,256]{5,4,3,2,1,0:T(8,128)S(1)}, f32[1,1,1,5,16,256]{5,4,3,2,1,0:T(8,128)}, u32[]{:S(2)}) %copy-start.1) | copy-done | bytes 81944
  3.9 0.0 copy-start.3
  3.9 0.9 %copy-done.3 = f32[16,16,256]{2,1,0:T(8,128)S(1)} copy-done((f32[16,16,256]{2,1,0:T(8,128)S(1)}, f32[16,16,256]{2,1,0:T(8,128)}, u32[]{:S(2)}) %copy-start.3) | copy-done | bytes 262168
  4.9 0.0 copy-start.4
  4.9 0.7 %copy-done.4 = f32[1,1,1,16,16]{4,3,2,1,0:T(8,128)S(1)} copy-done((f32[1,1,1,16,16]{4,3,2,1,0:T(8,128)S(1)}, f32[1,1,1,16,16]{4,3,2,1,0:T(8,128)}, u32[]{:S(2)}) %copy-start.4) | copy-done | bytes 1048
  5.6 12.9 %halo.1 = (f32[18,24,256]{2,1,0:T(8,128)S(1)}, f32[18,24,128]{2,1,0:T(8,128)S(1)}, f32[8,256]{1,0:T(8,128)S(1)}, f32[16,128]{1,0:T(8,128)S(1)}) custom-call(f32[16,16,256]{2,1,0:T(8,128)S(1)} %copy-done.3, f32[8,8,256]{2,1,0:T(8,128)S(1)} %tile.10.basis, f32[16,16]{1,0:T(8,128)S(1)} %bitcast.13, f32[5,16,256]{2,1,0:T(8,128)S(1)} %bitcast.11), custom_call_target="tpu_custom_call" | custom-call | tf_op jit(solution)/shard_map/halo/pallas_call | solution.py:451
  18.4 0.0 copy-start
  18.4 1.8 %copy-done = bf16[1152,1280]{1,0:T(8,128)(2,1)S(1)} copy-done((bf16[1152,1280]{1,0:T(8,128)(2,1)S(1)}, bf16[1152,1280]{1,0:T(8,128)(2,1)}, u32[]{:S(2)}) %copy-start) | copy-done | bytes 2949144
  20.3 7.2 %smooth.1.fold = f32[18,24,384]{2,1,0:T(8,128)S(1)} custom-call(f32[18,24,256]{2,1,0:T(8,128)S(1)} %get-tuple-element.9.grid_in, f32[18,24,128]{2,1,0:T(8,128)S(1)} %get-tuple-element.10.ends_in, bf16[3,10,10,128]{3,2,1,0:T(8,128)(2,1)S(1)} %bitcast.10, f32[3,10,128]{2,1,0:T(8,128)S(1)} %copy.11.eig, bf16[1152,1280]{1,0:T(8,128)(2,1)S(1)} %copy-done), custom_call_target="tpu_custom_call" | custom-call | tf_op jit(solution)/shard_map/smooth/pallas_call | solution.py:189
  27.5 0.0 copy-done.2
  27.5 8.5 %fold.1 = f32[16,16,256]{2,1,0:T(8,128)S(1)} custom-call(f32[18,24,384]{2,1,0:T(8,128)S(1)} %smooth.1.fold, f32[8,8,256]{2,1,0:T(8,128)S(1)} %tile.10.basis, f32[5,16,256]{2,1,0:T(8,128)S(1)} %bitcast.12, f32[8,256]{1,0:T(8,128)S(1)} %get-tuple-element.11.run, f32[16,128]{1,0:T(8,128)S(1)} %get-tuple-element.12.base), custom_call_target="tpu_custom_call" | custom-call | tf_op jit(solution)/shard_map/fold/pallas_call | solution.py:474
  36.0 0.7 %copy.17 = f32[16,16,256]{2,1,0:T(8,128)} copy(f32[16,16,256]{2,1,0:T(8,128)S(1)} %fold.1) | data formatting | bytes 524288
  (1 shorter events, 0.0 us)
Async XLA Ops:
  2.5 25.0 %copy-start.2 = (f32[1,1,1,5,16,256]{5,4,3,2,1,0:T(8,128)S(1)}, f32[1,1,1,5,16,256]{5,4,3,2,1,0:T(8,128)}, u32[]{:S(2)}) copy-start(f32[1,1,1,5,16,256]{5,4,3,2,1,0:T(8,128)} %param.12) | copy-start | bytes 245764
  3.0 0.9 %copy-start.1 = (f32[1,1,1,5,16,256]{5,4,3,2,1,0:T(8,128)S(1)}, f32[1,1,1,5,16,256]{5,4,3,2,1,0:T(8,128)}, u32[]{:S(2)}) copy-start(f32[1,1,1,5,16,256]{5,4,3,2,1,0:T(8,128)} %param.12) | copy-start | bytes 245764
  3.9 0.9 %copy-start.3 = (f32[16,16,256]{2,1,0:T(8,128)S(1)}, f32[16,16,256]{2,1,0:T(8,128)}, u32[]{:S(2)}) copy-start(f32[16,16,256]{2,1,0:T(8,128)} %res.1) | copy-start | bytes 786436
  4.9 0.7 %copy-start.4 = (f32[1,1,1,16,16]{4,3,2,1,0:T(8,128)S(1)}, f32[1,1,1,16,16]{4,3,2,1,0:T(8,128)}, u32[]{:S(2)}) copy-start(f32[1,1,1,16,16]{4,3,2,1,0:T(8,128)} %param.11) | copy-start | bytes 3076
  18.4 1.8 %copy-start = (bf16[1152,1280]{1,0:T(8,128)(2,1)S(1)}, bf16[1152,1280]{1,0:T(8,128)(2,1)}, u32[]{:S(2)}) copy-start(bf16[1152,1280]{1,0:T(8,128)(2,1)} %constant.2.clone.sel) | copy-start | bytes 8847364

commit v2 on v1

--- a/solution.py
+++ b/solution.py
@@ -2,7 +2,6 @@
 
 import jax
 import jax.numpy as jnp
-import numpy as np
 from jax import lax
 from jax.experimental import pallas as pl
 from jax.experimental.pallas import tpu as pltpu
@@ -15,21 +14,25 @@
 BF16 = jnp.bfloat16
 
 
-def selection(groups, count):
+def fill_selection(sel, first, last, groups, count):
     lanes = groups * count
     size = count * PTS
-    matrix = np.zeros((groups * size + 128, EXT * lanes), np.float32)
-    for g in range(groups):
-        for r in range(count):
-            for k in range(EXT):
-                z = PTS * r + k - 1
-                row = g * size + z
-                if z < 0:
-                    row = groups * size + 2 * g
-                elif z >= size:
-                    row = groups * size + 2 * g + 1
-                matrix[row, k * lanes + g * count + r] = 1
-    return matrix
+    column = lax.broadcasted_iota(jnp.int32, (1, EXT * lanes), 1)
+    element = column % lanes
+    g, r = element // count, element % count
+    z = PTS * r + column // lanes - 1
+    target = g * size + z
+    target = jnp.where(z < 0, groups * size + 2 * g, target)
+    target = jnp.where(z >= size, groups * size + 2 * g + 1, target)
+    target = jnp.broadcast_to(target, (ROWS, EXT * lanes))
+    row = lax.broadcasted_iota(jnp.int32, (ROWS, EXT * lanes), 0)
+
+    def body(n, _):
+        start = pl.multiple_of(n * ROWS, ROWS)
+        sel[pl.ds(start, ROWS), :] = jnp.where(row + start == target, 1.0, 0.0).astype(BF16)
+        return 0
+
+    lax.fori_loop(first // ROWS, last // ROWS, body, 0)
 
 
 def halves(value):
@@ -181,9 +184,8 @@
     scatter_elements(buf, sel, parts, grid_out, ends_out, ex, ey)
 
 
-def smooth_call(grid, ends, vectors, eigen, ex, ey, ez):
+def smooth_call(grid, ends, vectors, eigen, sel, ex, ey):
     nx, tall, size = grid.shape
-    sel = jnp.asarray(selection(ex * ey, ez), BF16)
     vmem = pl.BlockSpec(memory_space=pltpu.VMEM)
     rows = EXT * ROWS
     return pl.pallas_call(
@@ -199,7 +201,7 @@
             pltpu.VMEM((2 * EXT * 8, 128), F32),
             pltpu.VMEM((ROWS, 128), F32),
         ],
-        compiler_params=pltpu.CompilerParams(vmem_limit_bytes=40 * 1024 * 1024),
+        compiler_params=pltpu.CompilerParams(vmem_limit_bytes=20 * 1024 * 1024),
         name="smooth",
     )(grid, ends, vectors, eigen, sel)
 
@@ -286,14 +288,29 @@
     return [lax.axis_index(axis) for axis in AXES]
 
 
-def halo_kernel(sizes, bits, res, basis, own, sep, grid, ends, run, base, xin, yout, yin, zout, zin, slots, inbox,
+def halo_kernel(sizes, bits, res_far, basis_in, own_far, sep_far, grid, ends, run, base, basis, sel, res, own, sep, loaded, xin, yout, yin, zout, zin, slots, inbox,
                 sent, came, tree_sent, tree_came):
     cx, cy, size = res.shape
     nx, tall = cx + 2, grid.shape[1]
     here = place()
+    loads = [
+        pltpu.make_async_copy(far, near, loaded.at[n])
+        for n, (far, near) in enumerate(((res_far, res), (own_far, own), (sep_far, sep)))
+    ]
+    for load in loads:
+        load.start()
     for ref in (xin, yin, zin, grid, slots, yout):
         ref[...] = jnp.zeros_like(ref)
+    repeat = lax.broadcasted_iota(jnp.int32, (PTS, size), 1) % PTS == lax.broadcasted_iota(jnp.int32, (PTS, size), 0)
+    basis[...] = jnp.dot(
+        basis_in[...].reshape(PTS * PTS, PTS),
+        jnp.where(repeat, 1.0, 0.0),
+        precision=lax.Precision.HIGHEST,
+        preferred_element_type=F32,
+    ).reshape(basis.shape)
     greet(sizes, here, bits)
+    for load in loads:
+        load.wait()
     along_x = Sides(0, sizes, here, res.at[0], res.at[cx - 1], xin, sent, came)
     along_x.start()
 
@@ -317,6 +334,9 @@
     for x in range(cx):
         grid[x + 1, 1 : cy + 1, :] = res[x]
 
+    groups = (cx // PTS) * (cy // PTS)
+    cuts = [ROWS * (n * sel.shape[0] // (3 * ROWS)) for n in range(4)]
+    fill_selection(sel, cuts[0], cuts[1], groups, size // PTS)
     along_x.arrive()
     grid[0, 1 : cy + 1, :] = xin[0]
     grid[nx - 1, 1 : cy + 1, :] = xin[1]
@@ -327,6 +347,7 @@
     along_y.start()
     tree.step(0)
     tree.start(1)
+    fill_selection(sel, cuts[1], cuts[2], groups, size // PTS)
     along_y.arrive()
     for x in range(nx):
         grid[x, 0:1, :] = yin[0, x : x + 1, :]
@@ -345,6 +366,7 @@
     along_z.start()
     tree.step(1)
     tree.start(2)
+    fill_selection(sel, cuts[2], cuts[3], groups, size // PTS)
     along_z.arrive()
     row = lax.broadcasted_iota(jnp.int32, (8, padded), 0)
     head = jnp.where(row == 0, zin[0, 7:8, :], jnp.where(row == 1, zin[1, 0:1, :], 0.0))
@@ -431,7 +453,6 @@
     own = x_interior.reshape(x_interior.shape[3:])
     sep = x_separator.reshape(x_separator.shape[3:])
     levels, unknowns, width = sep.shape
-    basis = jnp.tile(coarse_basis, (1, 1, ez))
     bits = tree_bits(sizes)
     early = bits[:3]
     late = bits[3:]
@@ -440,6 +461,7 @@
     wide = -(-(nx * tall) // 128) * 128
     flat = -(-nx // 8) * 8
     vmem = pl.BlockSpec(memory_space=pltpu.VMEM)
+    far = pl.BlockSpec(memory_space=pltpu.HBM)
     dma = pltpu.SemaphoreType.DMA
 
     def tree_scratch(rounds):
@@ -448,17 +470,23 @@
     def semaphores(rounds):
         return [dma((6,)), dma((6,)), dma((max(rounds, 1),)), dma((max(rounds, 1),))]
 
-    grid, ends, run, base = pl.pallas_call(
+    grid, ends, run, base, basis, sel = pl.pallas_call(
         functools.partial(halo_kernel, sizes, early),
         out_shape=(
             jax.ShapeDtypeStruct((nx, tall, cz), F32),
             jax.ShapeDtypeStruct((nx, tall, 128), F32),
             jax.ShapeDtypeStruct((deep, width), F32),
             jax.ShapeDtypeStruct((unknowns, 128), F32),
+            jax.ShapeDtypeStruct((PTS, PTS, cz), F32),
+            jax.ShapeDtypeStruct((ex * ey * cz + 128, EXT * ex * ey * ez), BF16),
         ),
-        in_specs=[vmem] * 4,
-        out_specs=(vmem,) * 4,
+        in_specs=[far, vmem, far, far],
+        out_specs=(vmem,) * 6,
         scratch_shapes=[
+            pltpu.VMEM((cx, cy, cz), F32),
+            pltpu.VMEM(own.shape, F32),
+            pltpu.VMEM(sep.shape, F32),
+            dma((3,)),
             pltpu.VMEM((2, cy, cz), F32),
             pltpu.VMEM((2, flat, cz), F32),
             pltpu.VMEM((2, flat, cz), F32),
@@ -466,11 +494,11 @@
             pltpu.VMEM((2, 8, wide), F32),
         ] + tree_scratch(len(early)) + semaphores(len(early)),
         compiler_params=pltpu.CompilerParams(
-            collective_id=0, has_side_effects=True, vmem_limit_bytes=32 * 1024 * 1024
+            collective_id=0, has_side_effects=True, vmem_limit_bytes=12 * 1024 * 1024
         ),
         name="halo",
-    )(residual, basis, own, sep)
-    folded = smooth_call(grid, ends, vectors, eigen, ex, ey, ez)
+    )(residual, coarse_basis, own, sep)
+    folded = smooth_call(grid, ends, vectors, eigen, sel, ex, ey)
     return pl.pallas_call(
         functools.partial(fold_kernel, sizes, late, len(early)),
         out_shape=jax.ShapeDtypeStruct((cx, cy, cz), F32),
@@ -485,7 +513,7 @@
             pltpu.VMEM((2, 8, cx * tall), F32),
         ] + tree_scratch(len(late)) + semaphores(len(late)),
         compiler_params=pltpu.CompilerParams(
-            collective_id=1, has_side_effects=True, vmem_limit_bytes=32 * 1024 * 1024
+            collective_id=1, has_side_effects=True, vmem_limit_bytes=12 * 1024 * 1024
         ),
         name="fold",
     )(folded, basis, sep, run, base)

time: 37.1 us -> 34.8 us (0.938)
  local copies, waits for them, and re-layouts: 8.08 us -> 5.68 us
    another operation x2 -> x0, local copies, waits for them, and re-layouts: 1.36 us -> none  [on_device(): basis = jnp.tile(coarse_basis, (1, 1, ez))]
    unnamed x13, local copies, waits for them, and re-layouts: 6.71 us -> 5.67 us
where the time goes in v2:
time: 34.8 us; the launch traced here: 34.5 us
  Pallas kernels  28.8 us (83%)
  local copies, waits for them, and re-layouts  5.68 us (16%)
    pallas_call x1, Pallas kernels, on_device(): pl.pallas_call(functools.partial(halo_kernel, sizes, early), out_shape=(j...  13.2 us
    pallas_call x1, Pallas kernels, on_device(): pl.pallas_call(functools.partial(fold_kernel, sizes, late, len(early)), o...  8.35 us
    pallas_call x1, Pallas kernels, smooth_call(): pl.pallas_call(functools.partial(smooth_kernel, ex, ey), out_shape=jax.Sh...  7.25 us
    unnamed x13, local copies, waits for them, and re-layouts  5.67 us

profile of v2, /device:TPU:0, one launch (start us, length us, event | category | flops | bytes accessed | tf_op | source)
XLA Modules:
  0.0 34.5 jit_solution(1339384836405514340)
XLA Ops:
  0.0 0.0 copy-start.1
  0.0 0.8 %copy.14 = f32[1,1,1,3,10,128]{5,3,4,2,1,0:T(4,128)S(1)} copy(f32[1,1,1,3,10,128]{5,2,4,3,1,0:T(1,128)} %param.8) | data formatting | bytes 30720 | tf_op args[2]
  0.8 0.9 %copy.13 = bf16[1,1,1,3,10,10,128]{6,5,4,3,2,1,0:T(8,128)(2,1)S(1)} copy(bf16[1,1,1,3,10,10,128]{6,3,5,4,2,1,0:T(4,128)(2,1)} %param.7) | data formatting | bytes 153600 | tf_op args[1]
  1.7 0.0 copy-start
  1.7 0.9 %copy-done = f32[1,1,1,5,16,256]{5,4,3,2,1,0:T(8,128)S(1)} copy-done((f32[1,1,1,5,16,256]{5,4,3,2,1,0:T(8,128)S(1)}, f32[1,1,1,5,16,256]{5,4,3,2,1,0:T(8,128)}, u32[]{:S(2)}) %copy-start) | copy-done | bytes 81944
  2.6 0.0 copy-start.2
  2.6 0.9 %copy-done.2 = f32[16,16,256]{2,1,0:T(8,128)S(1)} copy-done((f32[16,16,256]{2,1,0:T(8,128)S(1)}, f32[16,16,256]{2,1,0:T(8,128)}, u32[]{:S(2)}) %copy-start.2) | copy-done | bytes 262168
  3.5 0.0 copy-start.3
  3.5 0.8 %copy-done.3 = f32[8,8,8]{2,1,0:T(8,128)S(1)} copy-done((f32[8,8,8]{2,1,0:T(8,128)S(1)}, f32[8,8,8]{2,1,0:T(8,128)}, u32[]{:S(2)}) %copy-start.3) | copy-done | bytes 2072
  4.3 0.0 copy-start.4
  4.3 0.7 %copy-done.4 = f32[1,1,1,16,16]{4,3,2,1,0:T(8,128)S(1)} copy-done((f32[1,1,1,16,16]{4,3,2,1,0:T(8,128)S(1)}, f32[1,1,1,16,16]{4,3,2,1,0:T(8,128)}, u32[]{:S(2)}) %copy-start.4) | copy-done | bytes 1048
  5.0 13.2 %halo.1 = (f32[18,24,256]{2,1,0:T(8,128)S(1)}, f32[18,24,128]{2,1,0:T(8,128)S(1)}, f32[8,256]{1,0:T(8,128)S(1)}, f32[16,128]{1,0:T(8,128)S(1)}, f32[8,8,256]{2,1...) custom-call(f32[16,16,256]{2,1,0:T(8,128)S(1)} %copy-done.2, f32[8,8,8]{2,1,0:T(8,128)S(1)} %copy-done.3, f32[16,16]{1,0:T(8,128)S(1)} %bitcast.11, ...), custom_call_target="tpu_custom_call" | custom-call | tf_op jit(solution)/shard_map/halo/pallas_call | solution.py:473
  18.2 7.2 %smooth.1.fold = f32[18,24,384]{2,1,0:T(8,128)S(1)} custom-call(f32[18,24,256]{2,1,0:T(8,128)S(1)} %get-tuple-element.11.grid_in, f32[18,24,128]{2,1,0:T(8,128)S(1)} %get-tuple-element.12.ends_in, bf16[3,10,10,128]{3,2,1,0:T(8,128)(2,1)S(1)} %bitcast.8, f32[3,10,128]{2,1,0:T(8,128)S(1)} %copy.10.eig, bf16[1152,1280]{1,0:T(8,128)(2,1)S(1)} %get-tuple-element.13.sel), custom_call_target="tpu_custom_call" | custom-call | tf_op jit(solution)/shard_map/smooth/pallas_call | solution.py:191
  25.4 0.0 copy-done.1
  25.4 8.4 %fold.1 = f32[16,16,256]{2,1,0:T(8,128)S(1)} custom-call(f32[18,24,384]{2,1,0:T(8,128)S(1)} %smooth.1.fold, f32[8,8,256]{2,1,0:T(8,128)S(1)} %get-tuple-element.14.basis, f32[5,16,256]{2,1,0:T(8,128)S(1)} %bitcast.10, f32[8,256]{1,0:T(8,128)S(1)} %get-tuple-element.15.run, f32[16,128]{1,0:T(8,128)S(1)} %get-tuple-element.16.base), custom_call_target="tpu_custom_call" | custom-call | tf_op jit(solution)/shard_map/fold/pallas_call | solution.py:502
  33.8 0.7 %copy.16 = f32[16,16,256]{2,1,0:T(8,128)} copy(f32[16,16,256]{2,1,0:T(8,128)S(1)} %fold.1) | data formatting | bytes 524288
  (1 shorter events, 0.0 us)
Async XLA Ops:
  0.0 25.4 %copy-start.1 = (f32[1,1,1,5,16,256]{5,4,3,2,1,0:T(8,128)S(1)}, f32[1,1,1,5,16,256]{5,4,3,2,1,0:T(8,128)}, u32[]{:S(2)}) copy-start(f32[1,1,1,5,16,256]{5,4,3,2,1,0:T(8,128)} %param.11) | copy-start | bytes 245764
  1.7 0.9 %copy-start = (f32[1,1,1,5,16,256]{5,4,3,2,1,0:T(8,128)S(1)}, f32[1,1,1,5,16,256]{5,4,3,2,1,0:T(8,128)}, u32[]{:S(2)}) copy-start(f32[1,1,1,5,16,256]{5,4,3,2,1,0:T(8,128)} %param.11) | copy-start | bytes 245764
  2.6 0.9 %copy-start.2 = (f32[16,16,256]{2,1,0:T(8,128)S(1)}, f32[16,16,256]{2,1,0:T(8,128)}, u32[]{:S(2)}) copy-start(f32[16,16,256]{2,1,0:T(8,128)} %res_far.1) | copy-start | bytes 786436
  3.5 0.8 %copy-start.3 = (f32[8,8,8]{2,1,0:T(8,128)S(1)}, f32[8,8,8]{2,1,0:T(8,128)}, u32[]{:S(2)}) copy-start(f32[8,8,8]{2,1,0:T(8,128)} %basis_in.1) | copy-start | bytes 6148
  4.3 0.7 %copy-start.4 = (f32[1,1,1,16,16]{4,3,2,1,0:T(8,128)S(1)}, f32[1,1,1,16,16]{4,3,2,1,0:T(8,128)}, u32[]{:S(2)}) copy-start(f32[1,1,1,16,16]{4,3,2,1,0:T(8,128)} %param.10) | copy-start | bytes 3076
